TPU v7x, 32 devices: a whole 2x2x4 slice. The times are simulated.
32 devices in a mesh: date: 2 (over x), trade: 16 (over z, y, core).
Axes of the slice: x: 2, y: 2, z: 4, core: 2. Of those that a mesh axis runs over, the one named last changes fastest.
Arguments:
- initial_term_structure: float32 [48], replicated, may hold values from 0.01 to 0.06
- long_level: float32 [48], replicated, may hold values from 0.01 to 0.07
- reversion: float32 [48], replicated, may hold values from 0.02 to 2
- volatility: float32 [48], replicated, may hold values from 0.002 to 0.01
- mixing: float32 [48, 48], replicated, may hold values from -0.875 to 0.875
- shocks: float32 [4, 48, 512], P('date'), may hold values from -6 to 6
- cashflows: bfloat16 [48, 131072], P(None, 'trade'), may hold values from -0.01953125 to 0.01953125
- maturity: int32 [131072], P('trade'), may hold values from 1 to 4, as said below
- netting: int32 [131072], P('trade'), may hold values from 0 to 63
Outputs:
- exposure: float32 [4, 64], P('date', 'trade')
Inputs may be any that keep to these rules, and one draw needn't show every extreme that they name: Trades are grouped by maturity along trade: the trades held by one device mature within a narrow band of dates that rises with the device's index.
All inputs are finite; a program needn't handle non-finite values.
Results may differ from a plain program's by a relative error of at most 0.003.
Values may be sent and summed in bfloat16 or wider, within the bound.
A program may use at most 64 MiB of HBM per device.

v0:
```python
import functools
import math

import jax
import jax.numpy as jnp
from jax import lax
from jax.experimental import pallas as pl
from jax.experimental.pallas import tpu as pltpu
from jax.sharding import PartitionSpec as P

SETS_DEV = 4
LANES = 128
MESH = pl.DeviceIdType.MESH


def each(count, body):
    if count <= 16:
        for index in range(count):
            body(index)
    else:
        pl.loop(0, count)(body)


def split(x):
    high = x.astype(jnp.bfloat16)
    low = (x - high.astype(jnp.float32)).astype(jnp.bfloat16)
    return high, low


def kernel(
    dates_dev,
    dates_n,
    trade_n,
    start_hbm,
    level_hbm,
    speed_hbm,
    vol_hbm,
    mixing_hbm,
    shocks_hbm,
    cash_hbm,
    maturity_hbm,
    netting_hbm,
    out_ref,
    start_ref,
    level_ref,
    speed_ref,
    vol_ref,
    mixing_ref,
    maturity_ref,
    netting_ref,
    shocks_v,
    cash_v,
    code_v,
    acc_v,
    offset_v,
    state_v,
    leave_v,
    arrive_v,
    send_v,
    recv_v,
    load_sem,
    cash_sem,
    leave_sem,
    arrive_sem,
    send_sem,
    recv_sem,
):
    factors, trades = cash_v.shape
    paths = shocks_v.shape[2]
    chunks = cash_sem.shape[0]
    chunk = trades // chunks
    sets_all = SETS_DEV * trade_n
    maturities = dates_dev * dates_n
    width = send_v.shape[2]
    date = lax.axis_index("date")
    me = lax.axis_index("trade")

    loads = [
        pltpu.make_async_copy(source, target, load_sem.at[place])
        for place, (source, target) in enumerate(
            (
                (shocks_hbm, shocks_v),
                (mixing_hbm, mixing_ref),
                (start_hbm, start_ref),
                (level_hbm, level_ref),
                (speed_hbm, speed_ref),
                (vol_hbm, vol_ref),
                (maturity_hbm, maturity_ref),
                (netting_hbm, netting_ref),
            )
        )
    ]
    for load in loads:
        load.start()

    def cash_copy(index):
        part = pl.ds(pl.multiple_of(index * chunk, chunk), chunk)
        return pltpu.make_async_copy(cash_hbm.at[:, part], cash_v.at[:, part], cash_sem.at[index])

    for index in range(chunks):
        cash_copy(index).start()

    barrier = pltpu.get_barrier_semaphore()

    def greet(index):
        other = lax.rem(me + 1 + index, trade_n)
        pl.semaphore_signal(barrier, inc=1, device_id={"trade": other}, device_id_type=MESH)

    each(trade_n - 1, greet)

    @pl.when(date > 0)
    def _():
        pl.semaphore_signal(barrier, inc=1, device_id={"date": date - 1}, device_id_type=MESH)

    for load in loads:
        load.wait()

    diagonal = lax.broadcasted_iota(jnp.int32, (factors, factors), 0) == lax.broadcasted_iota(
        jnp.int32, (factors, factors), 1
    )

    def column(ref):
        return jnp.sum(jnp.where(diagonal, ref[...], 0.0), axis=1, keepdims=True)

    decay = jnp.exp(-0.25 * column(speed_ref))
    drift = (1.0 - decay) * column(level_ref)
    start = jnp.broadcast_to(column(start_ref), (factors, paths))
    mix_high, mix_low = split(column(vol_ref) * mixing_ref[...])
    mix = jnp.concatenate([mix_high, mix_high, mix_low], axis=1)

    common = math.lcm(*range(1, maturities + 1))
    whole = common <= 256
    if whole:
        expiry = maturity_ref[...]
        share = jnp.zeros_like(expiry)
        for m in range(1, maturities + 1):
            share = jnp.where(expiry == m, common // m, share)
        code_v[dates_dev] = netting_ref[...].astype(jnp.float32)
        for step in range(dates_dev):
            left = jnp.maximum(expiry - (date * dates_dev + step), 0)
            code_v[step] = (share * left).astype(jnp.float32)
    else:
        for m in range(1, maturities + 1):
            code_v[m - 1] = jnp.where(maturity_ref[...] == m, netting_ref[...], -1).astype(
                jnp.float32
            )

    running = None
    power = jnp.ones_like(decay)
    for step in range(dates_dev):
        high, low = split(shocks_v[step])
        moved = jnp.dot(
            mix, jnp.concatenate([high, low, high], axis=0), preferred_element_type=jnp.float32
        )
        running = drift + moved if step == 0 else decay * running + drift + moved
        power = power * decay
        offset_v[step] = running

    leave_copy = pltpu.make_async_remote_copy(
        src_ref=leave_v,
        dst_ref=arrive_v,
        send_sem=leave_sem,
        recv_sem=arrive_sem,
        device_id={"date": date + 1},
        device_id_type=MESH,
    )

    def leave(state):
        leave_v[...] = (power * state + running).astype(jnp.bfloat16)
        leave_copy.start()

    tiles = sets_all // 16
    place = lax.broadcasted_iota(jnp.int32, (16, LANES), 0).astype(jnp.float32)
    marks = [(place + 16.0 * i).astype(jnp.bfloat16) for i in range(tiles)]
    one = jnp.ones((16, LANES), jnp.bfloat16)
    zero = jnp.zeros((16, LANES), jnp.bfloat16)
    rows = chunk // LANES

    def members(m, index):
        pieces = []
        for r in range(rows):
            code = jnp.broadcast_to(code_v[m, pl.ds(index * rows + r, 1), :], (16, LANES))
            code = code.astype(jnp.bfloat16)
            pieces.append(
                jnp.concatenate([jnp.where(code == mark, one, zero) for mark in marks], axis=0)
            )
        return jnp.concatenate(pieces, axis=1)

    def weighted(index):
        pieces = []
        for r in range(rows):
            spread = [
                jnp.broadcast_to(
                    code_v[step, pl.ds(index * rows + r, 1), :], (16, LANES)
                ).astype(jnp.bfloat16)
                for step in range(dates_dev + 1)
            ]
            same = [spread[-1] == mark for mark in marks]
            pieces.append(
                jnp.concatenate(
                    [jnp.where(here, share, zero) for share in spread[:-1] for here in same], axis=0
                )
            )
        return jnp.concatenate(pieces, axis=1)

    def summed(member, index, copies):
        cash = cash_v[:, pl.ds(pl.multiple_of(index * chunk, chunk), chunk)]
        cash = jnp.concatenate([cash] * copies, axis=0)
        return lax.dot_general(
            member, cash, (((1,), (1,)), ((), ())), preferred_element_type=jnp.float32
        )

    lane = lax.broadcasted_iota(jnp.int32, (1, dates_dev * factors), 1)
    at_date = date * dates_dev + lane // factors

    def weight(m):
        return jnp.maximum(m - at_date, 0).astype(jnp.float32) / jnp.full_like(
            at_date, m
        ).astype(jnp.float32)

    if whole:
        total = jnp.zeros((dates_dev * sets_all, factors), jnp.float32)
        for index in range(chunks):
            cash_copy(index).wait()
            total = total + summed(weighted(index), index, 1)
        total = total * (1.0 / common)
        held = jnp.concatenate(
            [total[step * sets_all : (step + 1) * sets_all] for step in range(dates_dev)], axis=1
        )
    else:
        acc_v[...] = jnp.zeros_like(acc_v)
        for index in range(chunks):
            cash_copy(index).wait()

        @pl.loop(0, chunks)
        def _(index):
            @pl.loop(0, maturities)
            def _(m):
                acc_v[...] += weight(m + 1) * summed(members(m, index), index, dates_dev)

        held = acc_v[...]

    send_v[...] = jnp.zeros_like(send_v)
    for owner in range(trade_n):
        send_v[owner, :, : dates_dev * factors] = held[owner * SETS_DEV : (owner + 1) * SETS_DEV]

    pl.semaphore_wait(barrier, trade_n - 1 + (date < dates_n - 1).astype(jnp.int32))

    @pl.when(date == 0)
    def _():
        state_v[...] = start
        leave(start)

    if dates_n > 2:

        @pl.when(jnp.logical_and(date > 0, date < dates_n - 1))
        def _():
            leave_copy.wait_recv()
            state = arrive_v[...].astype(jnp.float32)
            state_v[...] = state
            leave(state)

    def push(index):
        other = index + (index >= me).astype(jnp.int32)
        pltpu.make_async_remote_copy(
            src_ref=send_v.at[other],
            dst_ref=recv_v.at[me - (me > other).astype(jnp.int32)],
            send_sem=send_sem,
            recv_sem=recv_sem,
            device_id={"trade": other},
            device_id_type=MESH,
        ).start()

    each(trade_n - 1, push)

    @pl.when(date == dates_n - 1)
    def _():
        leave_copy.wait_recv()
        state_v[...] = arrive_v[...].astype(jnp.float32)

    tenor = 0.25 * (
        lax.broadcasted_iota(jnp.int32, (factors, 1), 0).astype(jnp.float32) + 1.0
    )
    discounts = []
    power = jnp.ones_like(decay)
    for step in range(dates_dev):
        power = power * decay
        now = power * state_v[...] + offset_v[step]
        discounts.append(jnp.exp(-now * tenor).astype(jnp.bfloat16))
    if width > dates_dev * factors:
        discounts.append(jnp.zeros((width - dates_dev * factors, paths), jnp.bfloat16))
    discount = jnp.concatenate(discounts, axis=0)

    everything = pltpu.make_async_copy(recv_v, recv_v, recv_sem)
    everything.wait()
    owned = send_v[me] + jnp.sum(recv_v[...], axis=0)
    lane = lax.broadcasted_iota(jnp.int32, owned.shape, 1) // factors
    owned = jnp.concatenate([jnp.where(lane == step, owned, 0.0) for step in range(dates_dev)], axis=0)
    high, low = split(owned)
    value = jnp.dot(high, discount, preferred_element_type=jnp.float32) + jnp.dot(
        low, discount, preferred_element_type=jnp.float32
    )
    mean = jnp.sum(jnp.maximum(value, 0.0), axis=1, keepdims=True) / paths
    pick = lax.broadcasted_iota(jnp.int32, (SETS_DEV, SETS_DEV), 0) == lax.broadcasted_iota(
        jnp.int32, (SETS_DEV, SETS_DEV), 1
    )
    for step in range(dates_dev):
        part = mean[step * SETS_DEV : (step + 1) * SETS_DEV]
        out_ref[step : step + 1, :] = jnp.sum(jnp.where(pick, part, 0.0), axis=0, keepdims=True)

    pltpu.make_async_copy(recv_v, recv_v, send_sem).wait()

    @pl.when(date < dates_n - 1)
    def _():
        leave_copy.wait_send()


def per_device(
    initial_term_structure,
    long_level,
    reversion,
    volatility,
    mixing,
    shocks,
    cashflows,
    maturity,
    netting,
):
    dates_dev, factors, paths = shocks.shape
    trades = cashflows.shape[1]
    dates_n = lax.axis_size("date")
    trade_n = lax.axis_size("trade")
    sets_all = SETS_DEV * trade_n
    width = -(-dates_dev * factors // LANES) * LANES
    chunks = max(1, trades // 2048)
    row = lambda x: x.reshape(1, factors)
    tall = lambda x: x.reshape(trades // LANES, LANES)
    keep = lambda x: pltpu.with_memory_space_constraint(x, pltpu.HBM)
    vmem = pl.BlockSpec(memory_space=pltpu.VMEM)
    hbm = pl.BlockSpec(memory_space=pltpu.HBM)
    return pl.pallas_call(
        functools.partial(kernel, dates_dev, dates_n, trade_n),
        out_shape=jax.ShapeDtypeStruct((dates_dev, SETS_DEV), jnp.float32),
        in_specs=[hbm] * 9,
        out_specs=vmem,
        scratch_shapes=[
            pltpu.VMEM((1, factors), jnp.float32),
            pltpu.VMEM((1, factors), jnp.float32),
            pltpu.VMEM((1, factors), jnp.float32),
            pltpu.VMEM((1, factors), jnp.float32),
            pltpu.VMEM((factors, factors), jnp.float32),
            pltpu.VMEM((trades // LANES, LANES), jnp.int32),
            pltpu.VMEM((trades // LANES, LANES), jnp.int32),
            pltpu.VMEM((dates_dev, factors, paths), jnp.float32),
            pltpu.VMEM((factors, trades), jnp.bfloat16),
            pltpu.VMEM((max(dates_dev + 1, dates_dev * dates_n), trades // LANES, LANES), jnp.float32),
            pltpu.VMEM((sets_all, dates_dev * factors), jnp.float32),
            pltpu.VMEM((dates_dev, factors, paths), jnp.float32),
            pltpu.VMEM((factors, paths), jnp.float32),
            pltpu.VMEM((factors, paths), jnp.bfloat16),
            pltpu.VMEM((factors, paths), jnp.bfloat16),
            pltpu.VMEM((trade_n, SETS_DEV, width), jnp.float32),
            pltpu.VMEM((trade_n - 1, SETS_DEV, width), jnp.float32),
            pltpu.SemaphoreType.DMA((8,)),
            pltpu.SemaphoreType.DMA((chunks,)),
            pltpu.SemaphoreType.DMA,
            pltpu.SemaphoreType.DMA,
            pltpu.SemaphoreType.DMA,
            pltpu.SemaphoreType.DMA,
        ],
        compiler_params=pltpu.CompilerParams(
            collective_id=0, has_side_effects=True, vmem_limit_bytes=24 * 1024 * 1024
        ),
    )(
        keep(row(initial_term_structure)),
        keep(row(long_level)),
        keep(row(reversion)),
        keep(row(volatility)),
        keep(mixing),
        keep(shocks),
        keep(cashflows),
        keep(tall(maturity)),
        keep(tall(netting)),
    )


def solution(mesh):
    return jax.shard_map(
        per_device,
        mesh=mesh,
        in_specs=(
            P(),
            P(),
            P(),
            P(),
            P(),
            P("date", None, None),
            P(None, "trade"),
            P("trade"),
            P("trade"),
        ),
        out_specs=P("date", "trade"),
        check_vma=False,
    )
```

profile of v0, /device:TPU:0, one launch (start us, length us, event | category | flops | bytes accessed | tf_op | source)
XLA Modules:
  0.0 11.5 jit_solution(3673730165113136210)
XLA Ops:
  0.0 10.9 %shard_map.91 = f32[2,4]{1,0:T(2,128)S(1)} custom-call(f32[1,48]{1,0:T(1,128)} %bitcast.8, f32[1,48]{1,0:T(1,128)} %bitcast.9, f32[1,48]{1,0:T(1,128)} %bitcast.10, f32[1,48]{1,0:T(1,128)} %bitcast.11, f32[48,48]{1,0:T(8,128)} %mixing_hbm.1, f32[2,48,512]{2,1,0:T(8,128)} %shocks_hbm.1, bf16[48,8192]{1,0:T(8,128)(2,1)} %cash_hbm.1, s32[64,128]{1,0:T(8,128)} %bitcast.6, ...), custom_call_target="tpu_custom_call" | custom-call | tf_op jit(solution)/shard_map/pallas_call | solution.py:341
  11.0 0.6 %copy.11 = f32[2,4]{1,0:T(2,128)} copy(f32[2,4]{1,0:T(2,128)S(1)} %shard_map.91) | data formatting | bytes 64
where the time goes:
time: 11.7 us; the launch traced here: 11.5 us
  Pallas kernels  10.9 us (93%)
  local copies, waits for them, and re-layouts  0.56 us (5%)
    pallas_call x1, Pallas kernels, per_device(): pl.pallas_call(functools.partial(kernel, dates_dev, dates_n, trade_n), ou...  10.9 us
    unnamed x1, local copies, waits for them, and re-layouts  0.56 us

commit v1 on v0

--- a/solution.py
+++ b/solution.py
@@ -332,7 +332,7 @@
     trade_n = lax.axis_size("trade")
     sets_all = SETS_DEV * trade_n
     width = -(-dates_dev * factors // LANES) * LANES
-    chunks = max(1, trades // 2048)
+    chunks = max(1, trades // 4096)
     row = lambda x: x.reshape(1, factors)
     tall = lambda x: x.reshape(trades // LANES, LANES)
     keep = lambda x: pltpu.with_memory_space_constraint(x, pltpu.HBM)

time: 11.7 us -> 10.9 us (0.932)
  Pallas kernels: 10.9 us -> 10.2 us
    pallas_call x1, Pallas kernels: 10.9 us -> 10.2 us  [per_device(): pl.pallas_call(functools.partial(kernel, dates_dev, dates_n, trade_n), ou...]
where the time goes in v1:
time: 10.9 us; the launch traced here: 10.8 us
  Pallas kernels  10.2 us (94%)
  local copies, waits for them, and re-layouts  0.56 us (5%)
    pallas_call x1, Pallas kernels, per_device(): pl.pallas_call(functools.partial(kernel, dates_dev, dates_n, trade_n), ou...  10.2 us
    unnamed x1, local copies, waits for them, and re-layouts  0.56 us

profile of v1, /device:TPU:0, one launch (start us, length us, event | category | flops | bytes accessed | tf_op | source)
XLA Modules:
  0.0 10.8 jit_solution(15429254028162988913)
XLA Ops:
  0.0 10.2 %shard_map.91 = f32[2,4]{1,0:T(2,128)S(1)} custom-call(f32[1,48]{1,0:T(1,128)} %bitcast.8, f32[1,48]{1,0:T(1,128)} %bitcast.9, f32[1,48]{1,0:T(1,128)} %bitcast.10, f32[1,48]{1,0:T(1,128)} %bitcast.11, f32[48,48]{1,0:T(8,128)} %mixing_hbm.1, f32[2,48,512]{2,1,0:T(8,128)} %shocks_hbm.1, bf16[48,8192]{1,0:T(8,128)(2,1)} %cash_hbm.1, s32[64,128]{1,0:T(8,128)} %bitcast.6, ...), custom_call_target="tpu_custom_call" | custom-call | tf_op jit(solution)/shard_map/pallas_call | solution.py:341
  10.2 0.6 %copy.11 = f32[2,4]{1,0:T(2,128)} copy(f32[2,4]{1,0:T(2,128)S(1)} %shard_map.91) | data formatting | bytes 64

commit v2 on v1

--- a/solution.py
+++ b/solution.py
@@ -112,21 +112,8 @@
     def _():
         pl.semaphore_signal(barrier, inc=1, device_id={"date": date - 1}, device_id_type=MESH)
 
-    for load in loads:
+    for load in loads[6:]:
         load.wait()
-
-    diagonal = lax.broadcasted_iota(jnp.int32, (factors, factors), 0) == lax.broadcasted_iota(
-        jnp.int32, (factors, factors), 1
-    )
-
-    def column(ref):
-        return jnp.sum(jnp.where(diagonal, ref[...], 0.0), axis=1, keepdims=True)
-
-    decay = jnp.exp(-0.25 * column(speed_ref))
-    drift = (1.0 - decay) * column(level_ref)
-    start = jnp.broadcast_to(column(start_ref), (factors, paths))
-    mix_high, mix_low = split(column(vol_ref) * mixing_ref[...])
-    mix = jnp.concatenate([mix_high, mix_high, mix_low], axis=1)
 
     common = math.lcm(*range(1, maturities + 1))
     whole = common <= 256
@@ -145,30 +132,6 @@
                 jnp.float32
             )
 
-    running = None
-    power = jnp.ones_like(decay)
-    for step in range(dates_dev):
-        high, low = split(shocks_v[step])
-        moved = jnp.dot(
-            mix, jnp.concatenate([high, low, high], axis=0), preferred_element_type=jnp.float32
-        )
-        running = drift + moved if step == 0 else decay * running + drift + moved
-        power = power * decay
-        offset_v[step] = running
-
-    leave_copy = pltpu.make_async_remote_copy(
-        src_ref=leave_v,
-        dst_ref=arrive_v,
-        send_sem=leave_sem,
-        recv_sem=arrive_sem,
-        device_id={"date": date + 1},
-        device_id_type=MESH,
-    )
-
-    def leave(state):
-        leave_v[...] = (power * state + running).astype(jnp.bfloat16)
-        leave_copy.start()
-
     tiles = sets_all // 16
     place = lax.broadcasted_iota(jnp.int32, (16, LANES), 0).astype(jnp.float32)
     marks = [(place + 16.0 * i).astype(jnp.bfloat16) for i in range(tiles)]
@@ -240,25 +203,14 @@
 
         held = acc_v[...]
 
-    send_v[...] = jnp.zeros_like(send_v)
+    if width > dates_dev * factors:
+        filler = jnp.zeros((sets_all, width - dates_dev * factors), jnp.float32)
+        held = jnp.concatenate([held, filler], axis=1)
     for owner in range(trade_n):
-        send_v[owner, :, : dates_dev * factors] = held[owner * SETS_DEV : (owner + 1) * SETS_DEV]
+        send_v[owner] = held[owner * SETS_DEV : (owner + 1) * SETS_DEV]
 
     pl.semaphore_wait(barrier, trade_n - 1 + (date < dates_n - 1).astype(jnp.int32))
 
-    @pl.when(date == 0)
-    def _():
-        state_v[...] = start
-        leave(start)
-
-    if dates_n > 2:
-
-        @pl.when(jnp.logical_and(date > 0, date < dates_n - 1))
-        def _():
-            leave_copy.wait_recv()
-            state = arrive_v[...].astype(jnp.float32)
-            state_v[...] = state
-            leave(state)
 
     def push(index):
         other = index + (index >= me).astype(jnp.int32)
@@ -272,6 +224,61 @@
         ).start()
 
     each(trade_n - 1, push)
+
+    for load in loads[:6]:
+        load.wait()
+
+    diagonal = lax.broadcasted_iota(jnp.int32, (factors, factors), 0) == lax.broadcasted_iota(
+        jnp.int32, (factors, factors), 1
+    )
+
+    def column(ref):
+        return jnp.sum(jnp.where(diagonal, ref[...], 0.0), axis=1, keepdims=True)
+
+    decay = jnp.exp(-0.25 * column(speed_ref))
+    drift = (1.0 - decay) * column(level_ref)
+    start = jnp.broadcast_to(column(start_ref), (factors, paths))
+    mix_high, mix_low = split(column(vol_ref) * mixing_ref[...])
+    mix = jnp.concatenate([mix_high, mix_high, mix_low], axis=1)
+
+    running = None
+    power = jnp.ones_like(decay)
+    for step in range(dates_dev):
+        high, low = split(shocks_v[step])
+        moved = jnp.dot(
+            mix, jnp.concatenate([high, low, high], axis=0), preferred_element_type=jnp.float32
+        )
+        running = drift + moved if step == 0 else decay * running + drift + moved
+        power = power * decay
+        offset_v[step] = running
+
+    leave_copy = pltpu.make_async_remote_copy(
+        src_ref=leave_v,
+        dst_ref=arrive_v,
+        send_sem=leave_sem,
+        recv_sem=arrive_sem,
+        device_id={"date": date + 1},
+        device_id_type=MESH,
+    )
+
+    def leave(state):
+        leave_v[...] = (power * state + running).astype(jnp.bfloat16)
+        leave_copy.start()
+
+    @pl.when(date == 0)
+    def _():
+        state_v[...] = start
+        leave(start)
+
+    if dates_n > 2:
+
+        @pl.when(jnp.logical_and(date > 0, date < dates_n - 1))
+        def _():
+            leave_copy.wait_recv()
+            state = arrive_v[...].astype(jnp.float32)
+            state_v[...] = state
+            leave(state)
+
 
     @pl.when(date == dates_n - 1)
     def _():

time: 10.9 us -> 10.8 us (level)
    pallas_call x1, Pallas kernels: 10.2 us -> 10.1 us  [per_device(): pl.pallas_call(functools.partial(kernel, dates_dev, dates_n, trade_n), ou...]
where the time goes in v2:
time: 10.8 us; the launch traced here: 10.6 us
  Pallas kernels  10.1 us (94%)
  local copies, waits for them, and re-layouts  0.56 us (5%)
    pallas_call x1, Pallas kernels, per_device(): pl.pallas_call(functools.partial(kernel, dates_dev, dates_n, trade_n), ou...  10.1 us
    unnamed x1, local copies, waits for them, and re-layouts  0.56 us

profile of v2, /device:TPU:0, one launch (start us, length us, event | category | flops | bytes accessed | tf_op | source)
XLA Modules:
  0.0 10.6 jit_solution(12092457638010252965)
XLA Ops:
  0.0 10.1 %shard_map.91 = f32[2,4]{1,0:T(2,128)S(1)} custom-call(f32[1,48]{1,0:T(1,128)} %bitcast.8, f32[1,48]{1,0:T(1,128)} %bitcast.9, f32[1,48]{1,0:T(1,128)} %bitcast.10, f32[1,48]{1,0:T(1,128)} %bitcast.11, f32[48,48]{1,0:T(8,128)} %mixing_hbm.1, f32[2,48,512]{2,1,0:T(8,128)} %shocks_hbm.1, bf16[48,8192]{1,0:T(8,128)(2,1)} %cash_hbm.1, s32[64,128]{1,0:T(8,128)} %bitcast.6, ...), custom_call_target="tpu_custom_call" | custom-call | tf_op jit(solution)/shard_map/pallas_call | solution.py:348
  10.1 0.6 %copy.11 = f32[2,4]{1,0:T(2,128)} copy(f32[2,4]{1,0:T(2,128)S(1)} %shard_map.91) | data formatting | bytes 64
